TPU v7x, 512 devices: a whole 4x4x16 slice. The times are simulated.
512 devices in a mesh: blk: 64 (over x_hi, z, core), help: 8 (over y, x_lo).
Axes of the slice: x: 4 (x_hi: 2, x_lo: 2; x = x_hi * 2 + x_lo), y: 4, z: 16, core: 2. Of those that a mesh axis runs over, the one named last changes fastest.
Arguments:
- features_t: bfloat16 [256, 98304], P(None, 'blk'), may hold values from -6 to 6
- weight: bfloat16 [256, 256], replicated, may hold values from -0.375 to 0.375
- bias: float32 [256], P('help'), may hold values from -3 to 3
- cotangent_t: bfloat16 [256, 98304], P('help', 'blk'), may hold values from -6 to 6
- tile_vals: bfloat16 [64, 8, 80, 128, 128], P('blk', 'help'), may hold values from -0.078125 to 0.078125
- slot_row: int32 [64, 8, 80], P('blk', 'help'), may hold values from 0 to 12, as said below
- slot_col: int32 [64, 8, 80], P('blk', 'help'), may hold values from 0 to 59, as said below
Outputs:
- output_t: bfloat16 [256, 98304], P('help', 'blk')
- propagated_grad: float32 [256, 98304], P('help', 'blk')
- weight_grad: float32 [256, 256], P(None, 'help')
- bias_grad: float32 [256], P('help')
Inputs may be any that keep to these rules, and one draw needn't show every extreme that they name: `slot_row`: each device has 80 slots, the used ones first; a slot holding 12 is unused. In every node-row block one helper uses all 80 slots and every other one at least 40. A slot's column tile is tile slot_col % 12 of node-row block (own block + slot_col // 12 - 2) taken around the loop of 64 blocks.
All inputs are finite; a program needn't handle non-finite values.
Results may differ from a plain program's by a relative error of at most 0.0045.
Values may be sent and summed in bfloat16 or wider, within the bound.
No kernel may reach another device: no remote copies, remote signals or barrier semaphores. Data moves between devices by JAX's collectives and lax.ppermute only.
A program may use at most 64 MiB of HBM per device.

v0:
```python
import math
import jax
import jax.numpy as jnp
from jax import lax
from jax.sharding import PartitionSpec as P

BAND = 2


def shifted(block, axis, distance):
    devices = range(lax.axis_size(axis))
    route = [((i - distance) % len(devices), i) for i in devices]
    return lax.ppermute(block, axis, route)


def gather_window(block):
    placed = []
    for offset in range(-BAND, BAND + 1):
        if offset == 0:
            placed.append(block)
        else:
            placed.append(shifted(block, "blk", -offset))
    stacked = jnp.stack(placed, axis=0)
    return stacked


def aggregate(stacked, tiles, rows, cols, row_tiles):
    tile = tiles.shape[-1]
    spans = stacked.shape[0]
    width = stacked.shape[1]
    banded = stacked.reshape(spans, width, row_tiles, tile)
    column_ids = jnp.arange(spans * row_tiles, dtype=jnp.int32).reshape(spans, row_tiles)
    picker = (cols[:, None, None] == column_ids[None, :, :]).astype(jnp.bfloat16)
    pieces = jnp.einsum("kbt,bftc->kfc", picker, banded, preferred_element_type=jnp.float32).astype(
        jnp.bfloat16
    )
    products = jnp.einsum("kfc,krc->kfr", pieces, tiles, preferred_element_type=jnp.float32)
    onehot = (rows[None, :] == jnp.arange(row_tiles, dtype=jnp.int32)[:, None]).astype(jnp.float32)
    summed = jnp.einsum("tk,kfr->ftr", onehot, products, precision=lax.Precision.HIGHEST)
    return summed.reshape(width, row_tiles * tile)


def per_device(features_t, weight, bias, cotangent_t, tile_vals, slot_row, slot_col):
    tiles = tile_vals[0, 0]
    rows = slot_row[0, 0]
    cols = slot_col[0, 0]
    tile = tiles.shape[-1]
    row_tiles = features_t.shape[1] // tile
    helper = lax.axis_index("help")
    share = cotangent_t.shape[0]
    partial_value = aggregate(gather_window(features_t), tiles, rows, cols, row_tiles)
    agg_share = lax.psum_scatter(partial_value, "help", scatter_dimension=0, tiled=True).astype(
        jnp.bfloat16
    )
    agg_full = lax.all_gather(agg_share, "help", axis=0, tiled=True)
    weight_cols = lax.dynamic_slice_in_dim(weight, helper * share, share, 1)
    pre = jnp.einsum("io,in->on", weight_cols, agg_full, preferred_element_type=jnp.float32)
    pre = pre + bias[:, None]
    output_t = jax.nn.elu(pre).astype(jnp.bfloat16)
    slope = jnp.where(pre > 0.0, jnp.ones_like(pre), jnp.exp(jnp.minimum(pre, 0.0)))
    grad_pre = (cotangent_t.astype(jnp.float32) * slope).astype(jnp.bfloat16)
    local_weight = jnp.einsum("in,on->io", agg_full, grad_pre, preferred_element_type=jnp.float32)
    local_bias = jnp.sum(grad_pre.astype(jnp.float32), axis=1)
    weight_sum, bias_sum = lax.psum((local_weight, local_bias), "blk")
    nodes_total = features_t.shape[1] * lax.axis_size("blk")
    scale = 1.0 / math.sqrt(nodes_total)
    grad_full = lax.all_gather(grad_pre, "help", axis=0, tiled=True)
    back = jnp.dot(weight, grad_full, preferred_element_type=jnp.float32).astype(jnp.bfloat16)
    back_partial = aggregate(gather_window(back), tiles, rows, cols, row_tiles)
    propagated = lax.psum_scatter(back_partial, "help", scatter_dimension=0, tiled=True)
    return (output_t, propagated, weight_sum * scale, bias_sum * scale)


def solution(mesh):
    placed = (
        P(None, "blk"),
        P(),
        P("help"),
        P("help", "blk"),
        P("blk", "help", None, None, None),
        P("blk", "help", None),
        P("blk", "help", None),
    )
    return jax.shard_map(
        per_device,
        mesh=mesh,
        in_specs=placed,
        out_specs=(P("help", "blk"), P("help", "blk"), P(None, "help"), P("help")),
        check_vma=False,
    )
```

profile of v0, /device:TPU:4, one launch (start us, length us, event | category | flops | bytes accessed | tf_op | source)
XLA Modules:
  0.0 542.9 jit_solution(9257986240852171921)
XLA Ops:
  7.2 1.6 copy.42
  8.8 11.3 %collective-permute-start.3 = (bf16[256,1536]{0,1:T(8,128)(2,1)S(1)}, bf16[256,1536]{0,1:T(8,128)(2,1)}, u32[]{:S(2)}, u32[]{:S(2)}) collective-permute-start(bf16[256,1536]{0,1:T(8,128)(2,1)S(1)} %copy.42), channel_id=1, source_target_pairs={{16,0},{24,8},{32,16},{40,24},{48,32},{56,40},{64,48},{72,56},{80,... | collective-permute-start | bytes 2359304 | tf_op jit(solution)/shard_map/ppermute | solution.py:13
  20.1 2.1 collective-permute-start.2
  22.2 2.3 collective-permute-start.1
  24.5 2.6 collective-permute-start
  27.1 1.8 copy.49
  28.9 8.1 %collective-permute-done.3 = bf16[256,1536]{0,1:T(8,128)(2,1)} collective-permute-done((bf16[256,1536]{0,1:T(8,128)(2,1)S(1)}, bf16[256,1536]{0,1:T(8,128)(2,1)}, u32[]{:S(2)}, u32[]{:S(2)}) %collective-permute-start.3) | collective-permute-done | bytes 786464 | tf_op jit(solution)/shard_map/ppermute | solution.py:13
  36.9 2.6 copy.51
  39.5 5.8 %collective-permute-done.2 = bf16[256,1536]{0,1:T(8,128)(2,1)} collective-permute-done((bf16[256,1536]{0,1:T(8,128)(2,1)S(1)}, bf16[256,1536]{0,1:T(8,128)(2,1)}, u32[]{:S(2)}, u32[]{:S(2)}) %collective-permute-start.2) | collective-permute-done | bytes 786464 | tf_op jit(solution)/shard_map/ppermute | solution.py:13
  45.3 2.6 copy.50
  48.0 2.6 copy.48
  50.6 2.9 copy.47
  53.6 1.5 constant_dynamic-update-slice_fusion.4
  55.1 1.5 constant_dynamic-update-slice_fusion.3
  56.6 1.5 constant_dynamic-update-slice_fusion.2
  58.6 1.6 bitcast_convert_fusion.1
  60.3 1.5 fusion.6
  61.8 23.6 %fusion.10 = f32[256,12,128]{2,1,0:T(8,128)} fusion(f32[80,256,128]{2,1,0:T(8,128)S(1)} %fusion.6, s32[80]{0:T(128)S(1)} %bitcast.54), kind=kOutput, calls=%fused_computation.14 | convolution fusion | flops 377488320 | bytes 12058944 | tf_op jit(solution)/shard_map/tk,kfr->ftr/dot_general | solution.py:39
  85.4 2.8 copy.54
  88.2 3.0 copy.67
  91.3 49.4 %reduce-scatter.7.cloned.1.call-done = f32[32,1536]{1,0:T(8,128)} async-done(((f32[256,1536]{1,0:T(8,128)}), f32[32,1536]{1,0:T(8,128)}) %reduce-scatter.7.cloned.1.call-update) | async-done | bytes 196624 | tf_op jit(solution)/shard_map/reduce_scatter | solution.py:52
  140.6 0.9 convert_element_type.32
  141.6 31.3 %all_gather.6 = bf16[256,1536]{1,0:T(8,128)(2,1)S(1)} all-gather(bf16[32,1536]{1,0:T(8,128)(2,1)S(1)} %convert_element_type.32), channel_id=1, replica_groups=mesh['blk'=64,'help'=8] {'help'}, dimensions={0}, use_global_device_ids=true | all-gather | bytes 884736 | tf_op jit(solution)/shard_map/all_gather | solution.py:55
  172.9 2.1 convert_reduce_fusion
  175.0 31.3 %all_gather.7 = bf16[256,1536]{1,0:T(8,128)(2,1)S(1)} all-gather(bf16[32,1536]{1,0:T(8,128)(2,1)S(1)} %get-tuple-element.19), channel_id=1, replica_groups=mesh['blk'=64,'help'=8] {'help'}, dimensions={0}, use_global_device_ids=true | all-gather | bytes 884736 | tf_op jit(solution)/shard_map/all_gather | solution.py:67
  206.3 2.2 convolution_convert_fusion
  208.5 1.9 collective-permute-start.6
  210.4 6.2 %collective-permute-start.7 = (bf16[256,1536]{0,1:T(8,128)(2,1)}, bf16[256,1536]{0,1:T(8,128)(2,1)}, u32[]{:S(2)}, u32[]{:S(2)}) collective-permute-start(bf16[256,1536]{0,1:T(8,128)(2,1)} %bitcast.14), channel_id=1, source_target_pairs={{16,0},{24,8},{32,16},{40,24},{48,32},{56,40},{64,48},{72,56},{80,... | collective-permute-start | bytes 2359304 | tf_op jit(solution)/shard_map/ppermute | solution.py:13
  216.6 2.1 collective-permute-start.5
  218.8 1.9 collective-permute-start.4
  220.7 2.6 copy.58
  223.3 2.6 copy.59
  225.9 13.2 %collective-permute-done.7 = bf16[256,1536]{0,1:T(8,128)(2,1)} collective-permute-done((bf16[256,1536]{0,1:T(8,128)(2,1)}, bf16[256,1536]{0,1:T(8,128)(2,1)}, u32[]{:S(2)}, u32[]{:S(2)}) %collective-permute-start.7) | collective-permute-done | bytes 786464 | tf_op jit(solution)/shard_map/ppermute | solution.py:13
  239.1 2.6 copy.60
  241.7 2.6 copy.57
  244.3 0.8 collective-permute-done.4
  245.1 2.6 copy.56
  247.7 1.6 constant_dynamic-update-slice_fusion.9
  249.2 1.5 constant_dynamic-update-slice_fusion.8
  250.7 1.5 constant_dynamic-update-slice_fusion.7
  252.7 1.6 bitcast_convert_fusion
  254.4 1.5 fusion.4
  255.9 10.9 %fusion.13 = f32[256,12,128]{2,1,0:T(8,128)} fusion(f32[80,256,128]{2,1,0:T(8,128)S(1)} %fusion.4, s32[80]{0:T(128)S(1)} %bitcast.55), kind=kOutput, calls=%fused_computation.15 | convolution fusion | flops 377488320 | bytes 12058944 | tf_op jit(solution)/shard_map/tk,kfr->ftr/dot_general | solution.py:39
  266.8 2.7 copy.63
  269.6 3.0 copy.69
  272.9 261.8 %all-reduce = (f32[256,32]{0,1:T(8,128)S(1)}, f32[32]{0:T(128)S(1)}) all-reduce(f32[256,32]{0,1:T(8,128)S(1)} %fusion.36, f32[32]{0:T(128)S(1)} %get-tuple-element.18), channel_id=1, replica_groups=mesh['blk'=64,'help'=8] {'blk'}, use_global_device_ids=true, to_apply=%region_2.3 | all-reduce | flops 8224 | bytes 65792 | tf_op jit(solution)/shard_map/psum | solution.py:64
  534.7 0.5 broadcast_multiply_fusion.1
  535.2 0.6 broadcast_multiply_fusion
  (31 shorter events, 1.5 us)
Async XLA Ops:
  7.2 53.1 %copy-start = (bf16[1,1,80,128,128]{4,3,2,1,0:T(8,128)(2,1)S(1)}, bf16[1,1,80,128,128]{4,3,2,1,0:T(8,128)(2,1)}, u32[]{:S(2)}) copy-start(bf16[1,1,80,128,128]{4,3,2,1,0:T(8,128)(2,1)} %param.11) | copy-start | bytes 7864324
  7.2 133.5 %reduce-scatter.7.cloned.1.call-start = ((), (), s32[]{:S(2)}) async-start(), calls=%async_computation.2 | async-start | bytes 1769472 | tf_op jit(solution)/shard_map/reduce_scatter | solution.py:52
  8.8 28.1 %collective-permute-start.3 = (bf16[256,1536]{0,1:T(8,128)(2,1)S(1)}, bf16[256,1536]{0,1:T(8,128)(2,1)}, u32[]{:S(2)}, u32[]{:S(2)}) collective-permute-start(bf16[256,1536]{0,1:T(8,128)(2,1)S(1)} %copy.42), channel_id=1, source_target_pairs={{16,0},{24,8},{32,16},{40,24},{48,32},{56,40},{64,48},{72,56},{80,... | collective-permute-start | bytes 2359304 | tf_op jit(solution)/shard_map/ppermute | solution.py:13
  20.1 25.2 %collective-permute-start.2 = (bf16[256,1536]{0,1:T(8,128)(2,1)S(1)}, bf16[256,1536]{0,1:T(8,128)(2,1)}, u32[]{:S(2)}, u32[]{:S(2)}) collective-permute-start(bf16[256,1536]{0,1:T(8,128)(2,1)S(1)} %copy.42), channel_id=1, source_target_pairs={{8,0},{16,8},{24,16},{32,24},{40,32},{48,40},{56,48},{64,56},{72,6... | collective-permute-start | bytes 2359304 | tf_op jit(solution)/shard_map/ppermute | solution.py:13
  22.2 25.7 %collective-permute-start.1 = (bf16[256,1536]{0,1:T(8,128)(2,1)S(1)}, bf16[256,1536]{0,1:T(8,128)(2,1)}, u32[]{:S(2)}, u32[]{:S(2)}) collective-permute-start(bf16[256,1536]{0,1:T(8,128)(2,1)S(1)} %copy.42), channel_id=1, source_target_pairs={{504,0},{0,8},{8,16},{16,24},{24,32},{32,40},{40,48},{48,56},{56,6... | collective-permute-start | bytes 2359304 | tf_op jit(solution)/shard_map/ppermute | solution.py:13
  24.5 26.1 %collective-permute-start = (bf16[256,1536]{0,1:T(8,128)(2,1)S(1)}, bf16[256,1536]{0,1:T(8,128)(2,1)}, u32[]{:S(2)}, u32[]{:S(2)}) collective-permute-start(bf16[256,1536]{0,1:T(8,128)(2,1)S(1)} %copy.42), channel_id=1, source_target_pairs={{496,0},{504,8},{0,16},{8,24},{16,32},{24,40},{32,48},{40,56},{48,... | collective-permute-start | bytes 2359304 | tf_op jit(solution)/shard_map/ppermute | solution.py:13
  53.5 4.5 copy-start.4
  53.5 4.8 copy-start.1
  53.5 5.1 copy-start.5
  60.3 1.6 copy-start.6
  85.4 87.5 %copy-start.7 = (f32[32]{0:T(128)S(1)}, f32[32]{0:T(128)}, u32[]{:S(2)}) copy-start(f32[32]{0:T(128)} %param.9) | copy-start | bytes 388
  91.2 444.6 %reduce-scatter.9.cloned.1.call-start = ((), (), s32[]{:S(2)}) async-start(), calls=%async_computation.3 | async-start | bytes 1769472
  208.5 14.8 %collective-permute-start.6 = (bf16[256,1536]{0,1:T(8,128)(2,1)}, bf16[256,1536]{0,1:T(8,128)(2,1)}, u32[]{:S(2)}, u32[]{:S(2)}) collective-permute-start(bf16[256,1536]{0,1:T(8,128)(2,1)} %bitcast.14), channel_id=1, source_target_pairs={{8,0},{16,8},{24,16},{32,24},{40,32},{48,40},{56,48},{64,56},{72,6... | collective-permute-start | bytes 2359304 | tf_op jit(solution)/shard_map/ppermute | solution.py:13
  210.4 28.7 %collective-permute-start.7 = (bf16[256,1536]{0,1:T(8,128)(2,1)}, bf16[256,1536]{0,1:T(8,128)(2,1)}, u32[]{:S(2)}, u32[]{:S(2)}) collective-permute-start(bf16[256,1536]{0,1:T(8,128)(2,1)} %bitcast.14), channel_id=1, source_target_pairs={{16,0},{24,8},{32,16},{40,24},{48,32},{56,40},{64,48},{72,56},{80,... | collective-permute-start | bytes 2359304 | tf_op jit(solution)/shard_map/ppermute | solution.py:13
  216.6 25.0 %collective-permute-start.5 = (bf16[256,1536]{0,1:T(8,128)(2,1)}, bf16[256,1536]{0,1:T(8,128)(2,1)}, u32[]{:S(2)}, u32[]{:S(2)}) collective-permute-start(bf16[256,1536]{0,1:T(8,128)(2,1)} %bitcast.14), channel_id=1, source_target_pairs={{504,0},{0,8},{8,16},{16,24},{24,32},{32,40},{40,48},{48,56},{56,6... | collective-permute-start | bytes 2359304 | tf_op jit(solution)/shard_map/ppermute | solution.py:13
  218.8 26.3 %collective-permute-start.4 = (bf16[256,1536]{0,1:T(8,128)(2,1)}, bf16[256,1536]{0,1:T(8,128)(2,1)}, u32[]{:S(2)}, u32[]{:S(2)}) collective-permute-start(bf16[256,1536]{0,1:T(8,128)(2,1)} %bitcast.14), channel_id=1, source_target_pairs={{496,0},{504,8},{0,16},{8,24},{16,32},{24,40},{32,48},{40,56},{48,... | collective-permute-start | bytes 2359304 | tf_op jit(solution)/shard_map/ppermute | solution.py:13
  247.7 4.5 copy-start.2
  247.7 4.8 copy-start.3
Sparse Core Ops, SparseCore 0:
  91.4 49.2 reduce-scatter.6
  272.7 50.2 reduce-scatter.8
where the time goes:
time: 546 us; the launch traced here: 543 us
  blocking collectives  324 us (59%)
  waiting for transfers between devices  77.3 us (14%)
  local copies, waits for them, and re-layouts  48.6 us (9%)
  matrix products  45.4 us (8%)
  starting transfers between devices  30.5 us (6%)
  between operations  14.5 us (3%)
    psum x1, blocking collectives, per_device(): weight_sum, bias_sum = lax.psum((local_weight, local_bias), 'blk')  262 us
    reduce_scatter x1, waiting for transfers between devices, per_device(): lax.psum_scatter(partial_value, 'help', scatter_dimension=0, tiled=True)  49.4 us
    dot_general x2, matrix products, aggregate(): jnp.einsum('tk,kfr->ftr', onehot, products, precision=lax.Precision.HIGHEST)  34.5 us
    all_gather x1, blocking collectives, per_device(): agg_full = lax.all_gather(agg_share, 'help', axis=0, tiled=True)  31.3 us
    all_gather x1, blocking collectives, per_device(): grad_full = lax.all_gather(grad_pre, 'help', axis=0, tiled=True)  31.3 us
    ppermute x8, starting transfers between devices, shifted(): return lax.ppermute(block, axis, route)  30.5 us
    ppermute x8, waiting for transfers between devices, shifted(): return lax.ppermute(block, axis, route)  27.9 us
    another operation x12, local copies, waits for them, and re-layouts, gather_window(): stacked = jnp.stack(placed, axis=0)  26 us
  transfers between devices with their start and end apart: 10, of which 5 were waited for; matrix products, arithmetic and copies ran while one was open for 4% of the time, Pallas kernels for 0%

commit v1 on v0

--- a/solution.py
+++ b/solution.py
@@ -64,7 +64,9 @@
     weight_sum, bias_sum = lax.psum((local_weight, local_bias), "blk")
     nodes_total = features_t.shape[1] * lax.axis_size("blk")
     scale = 1.0 / math.sqrt(nodes_total)
-    grad_full = lax.all_gather(grad_pre, "help", axis=0, tiled=True)
+    grad_full = jnp.concatenate(
+        lax.all_to_all(jnp.stack([grad_pre] * lax.axis_size("help")), "help", 0, 0), axis=0
+    )
     back = jnp.dot(weight, grad_full, preferred_element_type=jnp.float32).astype(jnp.bfloat16)
     back_partial = aggregate(gather_window(back), tiles, rows, cols, row_tiles)
     propagated = lax.psum_scatter(back_partial, "help", scatter_dimension=0, tiled=True)

time: 546 us -> 529 us (0.969)
  the two profiles are of different devices: /device:TPU:4 before, /device:TPU:2 now
where the time goes in v1:
time: 529 us; the launch traced here: 526 us
  blocking collectives  308 us (58%)
  waiting for transfers between devices  74.4 us (14%)
  local copies, waits for them, and re-layouts  48.7 us (9%)
  matrix products  45.5 us (9%)
  starting transfers between devices  33.1 us (6%)
  between operations  14.5 us (3%)
    psum x1, blocking collectives, per_device(): weight_sum, bias_sum = lax.psum((local_weight, local_bias), 'blk')  262 us
    reduce_scatter x1, waiting for transfers between devices, per_device(): lax.psum_scatter(partial_value, 'help', scatter_dimension=0, tiled=True)  46.4 us
    dot_general x2, matrix products, aggregate(): jnp.einsum('tk,kfr->ftr', onehot, products, precision=lax.Precision.HIGHEST)  34.5 us
    ppermute x8, starting transfers between devices, shifted(): return lax.ppermute(block, axis, route)  33 us
    all_gather x1, blocking collectives, per_device(): agg_full = lax.all_gather(agg_share, 'help', axis=0, tiled=True)  31.4 us
    ppermute x8, waiting for transfers between devices, shifted(): return lax.ppermute(block, axis, route)  27.9 us
    another operation x12, local copies, waits for them, and re-layouts, gather_window(): stacked = jnp.stack(placed, axis=0)  26 us
    unnamed x27, local copies, waits for them, and re-layouts  17.2 us
  transfers between devices with their start and end apart: 10, of which 5 were waited for; matrix products, arithmetic and copies ran while one was open for 4% of the time, Pallas kernels for 0%

profile of v1, /device:TPU:2, one launch (start us, length us, event | category | flops | bytes accessed | tf_op | source)
XLA Modules:
  0.0 525.7 jit_solution(14979162736208784026)
XLA Ops:
  7.2 1.6 copy.42
  8.8 13.0 %collective-permute-start.3 = (bf16[256,1536]{0,1:T(8,128)(2,1)S(1)}, bf16[256,1536]{0,1:T(8,128)(2,1)}, u32[]{:S(2)}, u32[]{:S(2)}) collective-permute-start(bf16[256,1536]{0,1:T(8,128)(2,1)S(1)} %copy.42), channel_id=1, source_target_pairs={{16,0},{24,8},{32,16},{40,24},{48,32},{56,40},{64,48},{72,56},{80,... | collective-permute-start | bytes 2359304 | tf_op jit(solution)/shard_map/ppermute | solution.py:13
  21.8 2.1 collective-permute-start.2
  23.8 2.3 collective-permute-start.1
  26.1 2.6 collective-permute-start
  28.7 1.8 copy.49
  30.5 8.1 %collective-permute-done.3 = bf16[256,1536]{0,1:T(8,128)(2,1)} collective-permute-done((bf16[256,1536]{0,1:T(8,128)(2,1)S(1)}, bf16[256,1536]{0,1:T(8,128)(2,1)}, u32[]{:S(2)}, u32[]{:S(2)}) %collective-permute-start.3) | collective-permute-done | bytes 786464 | tf_op jit(solution)/shard_map/ppermute | solution.py:13
  38.5 2.6 copy.51
  41.1 5.8 %collective-permute-done.2 = bf16[256,1536]{0,1:T(8,128)(2,1)} collective-permute-done((bf16[256,1536]{0,1:T(8,128)(2,1)S(1)}, bf16[256,1536]{0,1:T(8,128)(2,1)}, u32[]{:S(2)}, u32[]{:S(2)}) %collective-permute-start.2) | collective-permute-done | bytes 786464 | tf_op jit(solution)/shard_map/ppermute | solution.py:13
  47.0 2.6 copy.50
  49.6 2.6 copy.48
  52.2 2.9 copy.47
  55.2 1.5 constant_dynamic-update-slice_fusion.4
  56.7 1.5 constant_dynamic-update-slice_fusion.3
  58.2 1.5 constant_dynamic-update-slice_fusion.2
  60.2 1.6 bitcast_convert_fusion.1
  61.9 1.5 fusion.6
  63.4 23.6 %fusion.10 = f32[256,12,128]{2,1,0:T(8,128)} fusion(f32[80,256,128]{2,1,0:T(8,128)S(1)} %fusion.6, s32[80]{0:T(128)S(1)} %bitcast.56), kind=kOutput, calls=%fused_computation.14 | convolution fusion | flops 377488320 | bytes 12058944 | tf_op jit(solution)/shard_map/tk,kfr->ftr/dot_general | solution.py:39
  87.0 2.8 copy.54
  89.8 3.0 copy.67
  92.9 46.4 %reduce-scatter.7.cloned.1.call-done = f32[32,1536]{1,0:T(8,128)} async-done(((f32[256,1536]{1,0:T(8,128)}), f32[32,1536]{1,0:T(8,128)}) %reduce-scatter.7.cloned.1.call-update) | async-done | bytes 196624 | tf_op jit(solution)/shard_map/reduce_scatter | solution.py:52
  139.3 0.9 convert_element_type.32
  140.3 31.4 %all_gather.3 = bf16[256,1536]{1,0:T(8,128)(2,1)S(1)} all-gather(bf16[32,1536]{1,0:T(8,128)(2,1)S(1)} %convert_element_type.32), channel_id=1, replica_groups=mesh['blk'=64,'help'=8] {'help'}, dimensions={0}, use_global_device_ids=true | all-gather | bytes 884736 | tf_op jit(solution)/shard_map/all_gather | solution.py:55
  171.7 2.1 convert_reduce_fusion
  173.8 14.4 %all_to_all.5 = bf16[8,32,1536]{2,1,0:T(8,128)(2,1)S(1)} all-to-all(bf16[8,32,1536]{2,1,0:T(8,128)(2,1)S(1)} %stack.53), channel_id=1, replica_groups=mesh['blk'=64,'help'=8] {'help'}, dimensions={0} | all-to-all | bytes 1572864 | tf_op jit(solution)/shard_map/all_to_all | solution.py:68
  188.2 2.2 convolution_convert_fusion
  190.5 1.9 collective-permute-start.6
  192.4 7.1 %collective-permute-start.7 = (bf16[256,1536]{0,1:T(8,128)(2,1)}, bf16[256,1536]{0,1:T(8,128)(2,1)}, u32[]{:S(2)}, u32[]{:S(2)}) collective-permute-start(bf16[256,1536]{0,1:T(8,128)(2,1)} %bitcast.15), channel_id=1, source_target_pairs={{16,0},{24,8},{32,16},{40,24},{48,32},{56,40},{64,48},{72,56},{80,... | collective-permute-start | bytes 2359304 | tf_op jit(solution)/shard_map/ppermute | solution.py:13
  199.5 2.1 collective-permute-start.5
  201.6 1.9 collective-permute-start.4
  203.6 2.6 copy.58
  206.2 2.6 copy.59
  208.8 11.8 %collective-permute-done.7 = bf16[256,1536]{0,1:T(8,128)(2,1)} collective-permute-done((bf16[256,1536]{0,1:T(8,128)(2,1)}, bf16[256,1536]{0,1:T(8,128)(2,1)}, u32[]{:S(2)}, u32[]{:S(2)}) %collective-permute-start.7) | collective-permute-done | bytes 786464 | tf_op jit(solution)/shard_map/ppermute | solution.py:13
  220.6 2.6 copy.60
  223.2 2.6 copy.57
  225.8 2.2 collective-permute-done.4
  227.9 2.6 copy.56
  230.5 1.6 constant_dynamic-update-slice_fusion.9
  232.1 1.5 constant_dynamic-update-slice_fusion.8
  233.6 1.5 constant_dynamic-update-slice_fusion.7
  235.6 1.6 bitcast_convert_fusion
  237.2 1.5 fusion.4
  238.8 10.9 %fusion.13 = f32[256,12,128]{2,1,0:T(8,128)} fusion(f32[80,256,128]{2,1,0:T(8,128)S(1)} %fusion.4, s32[80]{0:T(128)S(1)} %bitcast.57), kind=kOutput, calls=%fused_computation.15 | convolution fusion | flops 377488320 | bytes 12058944 | tf_op jit(solution)/shard_map/tk,kfr->ftr/dot_general | solution.py:39
  249.7 2.7 copy.63
  252.4 3.0 copy.69
  255.8 261.7 %all-reduce = (f32[256,32]{0,1:T(8,128)S(1)}, f32[32]{0:T(128)S(1)}) all-reduce(f32[256,32]{0,1:T(8,128)S(1)} %fusion.36, f32[32]{0:T(128)S(1)} %get-tuple-element.18), channel_id=1, replica_groups=mesh['blk'=64,'help'=8] {'blk'}, use_global_device_ids=true, to_apply=%region_2.3 | all-reduce | flops 8224 | bytes 65792 | tf_op jit(solution)/shard_map/psum | solution.py:64
  517.5 0.5 broadcast_multiply_fusion.1
  518.0 0.6 broadcast_multiply_fusion
  (32 shorter events, 1.6 us)
Async XLA Ops:
  7.2 54.7 %copy-start = (bf16[1,1,80,128,128]{4,3,2,1,0:T(8,128)(2,1)S(1)}, bf16[1,1,80,128,128]{4,3,2,1,0:T(8,128)(2,1)}, u32[]{:S(2)}) copy-start(bf16[1,1,80,128,128]{4,3,2,1,0:T(8,128)(2,1)} %param.11) | copy-start | bytes 7864324
  7.2 132.2 %reduce-scatter.7.cloned.1.call-start = ((), (), s32[]{:S(2)}) async-start(), calls=%async_computation.3 | async-start | bytes 1769472 | tf_op jit(solution)/shard_map/reduce_scatter | solution.py:52
  8.8 29.8 %collective-permute-start.3 = (bf16[256,1536]{0,1:T(8,128)(2,1)S(1)}, bf16[256,1536]{0,1:T(8,128)(2,1)}, u32[]{:S(2)}, u32[]{:S(2)}) collective-permute-start(bf16[256,1536]{0,1:T(8,128)(2,1)S(1)} %copy.42), channel_id=1, source_target_pairs={{16,0},{24,8},{32,16},{40,24},{48,32},{56,40},{64,48},{72,56},{80,... | collective-permute-start | bytes 2359304 | tf_op jit(solution)/shard_map/ppermute | solution.py:13
  21.8 25.2 %collective-permute-start.2 = (bf16[256,1536]{0,1:T(8,128)(2,1)S(1)}, bf16[256,1536]{0,1:T(8,128)(2,1)}, u32[]{:S(2)}, u32[]{:S(2)}) collective-permute-start(bf16[256,1536]{0,1:T(8,128)(2,1)S(1)} %copy.42), channel_id=1, source_target_pairs={{8,0},{16,8},{24,16},{32,24},{40,32},{48,40},{56,48},{64,56},{72,6... | collective-permute-start | bytes 2359304 | tf_op jit(solution)/shard_map/ppermute | solution.py:13
  23.8 25.7 %collective-permute-start.1 = (bf16[256,1536]{0,1:T(8,128)(2,1)S(1)}, bf16[256,1536]{0,1:T(8,128)(2,1)}, u32[]{:S(2)}, u32[]{:S(2)}) collective-permute-start(bf16[256,1536]{0,1:T(8,128)(2,1)S(1)} %copy.42), channel_id=1, source_target_pairs={{504,0},{0,8},{8,16},{16,24},{24,32},{32,40},{40,48},{48,56},{56,6... | collective-permute-start | bytes 2359304 | tf_op jit(solution)/shard_map/ppermute | solution.py:13
  26.1 26.1 %collective-permute-start = (bf16[256,1536]{0,1:T(8,128)(2,1)S(1)}, bf16[256,1536]{0,1:T(8,128)(2,1)}, u32[]{:S(2)}, u32[]{:S(2)}) collective-permute-start(bf16[256,1536]{0,1:T(8,128)(2,1)S(1)} %copy.42), channel_id=1, source_target_pairs={{496,0},{504,8},{0,16},{8,24},{16,32},{24,40},{32,48},{40,56},{48,... | collective-permute-start | bytes 2359304 | tf_op jit(solution)/shard_map/ppermute | solution.py:13
  55.1 4.5 copy-start.4
  55.2 4.8 copy-start.1
  55.2 5.1 copy-start.5
  61.9 1.6 copy-start.6
  87.0 84.6 %copy-start.7 = (f32[32]{0:T(128)S(1)}, f32[32]{0:T(128)}, u32[]{:S(2)}) copy-start(f32[32]{0:T(128)} %param.9) | copy-start | bytes 388
  92.9 425.8 %reduce-scatter.9.cloned.1.call-start = ((), (), s32[]{:S(2)}) async-start(), calls=%async_computation.4 | async-start | bytes 1769472
  190.5 15.7 %collective-permute-start.6 = (bf16[256,1536]{0,1:T(8,128)(2,1)}, bf16[256,1536]{0,1:T(8,128)(2,1)}, u32[]{:S(2)}, u32[]{:S(2)}) collective-permute-start(bf16[256,1536]{0,1:T(8,128)(2,1)} %bitcast.15), channel_id=1, source_target_pairs={{8,0},{16,8},{24,16},{32,24},{40,32},{48,40},{56,48},{64,56},{72,6... | collective-permute-start | bytes 2359304 | tf_op jit(solution)/shard_map/ppermute | solution.py:13
  192.4 28.2 %collective-permute-start.7 = (bf16[256,1536]{0,1:T(8,128)(2,1)}, bf16[256,1536]{0,1:T(8,128)(2,1)}, u32[]{:S(2)}, u32[]{:S(2)}) collective-permute-start(bf16[256,1536]{0,1:T(8,128)(2,1)} %bitcast.15), channel_id=1, source_target_pairs={{16,0},{24,8},{32,16},{40,24},{48,32},{56,40},{64,48},{72,56},{80,... | collective-permute-start | bytes 2359304 | tf_op jit(solution)/shard_map/ppermute | solution.py:13
  199.5 23.7 %collective-permute-start.5 = (bf16[256,1536]{0,1:T(8,128)(2,1)}, bf16[256,1536]{0,1:T(8,128)(2,1)}, u32[]{:S(2)}, u32[]{:S(2)}) collective-permute-start(bf16[256,1536]{0,1:T(8,128)(2,1)} %bitcast.15), channel_id=1, source_target_pairs={{504,0},{0,8},{8,16},{16,24},{24,32},{32,40},{40,48},{48,56},{56,6... | collective-permute-start | bytes 2359304 | tf_op jit(solution)/shard_map/ppermute | solution.py:13
  201.6 26.3 %collective-permute-start.4 = (bf16[256,1536]{0,1:T(8,128)(2,1)}, bf16[256,1536]{0,1:T(8,128)(2,1)}, u32[]{:S(2)}, u32[]{:S(2)}) collective-permute-start(bf16[256,1536]{0,1:T(8,128)(2,1)} %bitcast.15), channel_id=1, source_target_pairs={{496,0},{504,8},{0,16},{8,24},{16,32},{24,40},{32,48},{40,56},{48,... | collective-permute-start | bytes 2359304 | tf_op jit(solution)/shard_map/ppermute | solution.py:13
  230.5 4.5 copy-start.2
  230.5 4.8 copy-start.3
Sparse Core Ops, SparseCore 0:
  93.0 46.2 reduce-scatter.6
  255.6 48.0 reduce-scatter.8
